TPU v7x, 512 devices: a whole 4x8x8 slice. The times are simulated.
512 devices in a mesh: prompt: 8 (over y), resp: 64 (over z, x, core).
Axes of the slice: x: 4, y: 8, z: 8, core: 2. Of those that a mesh axis runs over, the one named last changes fastest.
Arguments:
- queries: bfloat16 [8, 64, 256, 2048], P('prompt', 'resp')
- resp_kv: bfloat16 [8, 64, 256, 1024], P('prompt', 'resp')
- out_grad: bfloat16 [8, 64, 256, 2048], P('prompt', 'resp'), may hold values from -6 to 6
- prompt_kv: bfloat16 [64, 128, 1024], P('resp', 'prompt'), may hold values from -6 to 6
- prompt_of: int32 [64], replicated, may hold values from 0 to 63, as said below
- lengths: int32 [8, 64], P('prompt', 'resp'), may hold values from 1 to 2
Outputs:
- query_grad: bfloat16 [8, 64, 256, 2048], P('prompt', 'resp')
- resp_kv_grad: bfloat16 [8, 64, 256, 1024], P('prompt', 'resp')
- prompt_kv_grad: float32 [64, 128, 1024], P('resp', 'prompt')
Inputs may be any that keep to these rules, and one draw needn't show every extreme that they name: The cyclic distance between b and prompt_of[b] (mod 64) is at most 3; it is 3 on both sides for some b.
All inputs are finite; a program needn't handle non-finite values.
Results may differ from a plain program's by a relative error of at most 0.024.
Values may be sent and summed in bfloat16 or wider, within the bound.
A program may use at most 64 MiB of HBM per device.

v0:
```python
import jax
import jax.numpy as jnp
from jax import lax
from jax.sharding import PartitionSpec as P

QH = 16
KVH = 4
HD = 128
BLOCK = 128
REACH = 3
masked_value = -1e30


def from_behind(value, axis, steps):
    count = lax.axis_size(axis)
    pairs = [(source, (source + steps) % count) for source in range(count)]
    return lax.ppermute(value, axis, pairs)


def shards(queries, resp_kv, out_grad, prompt_kv, prompt_of, lengths):
    groups = QH // KVH
    softmax_scale = HD ** (-0.5)
    key_width = KVH * HD
    column = lax.axis_index("resp")
    group_size = lax.axis_size("resp")
    wanted = prompt_of[column]
    offset = (column - wanted + group_size + REACH) % group_size - REACH
    own_rows = prompt_kv[0]
    full_rows = lax.all_gather(own_rows, "prompt", axis=0, tiled=True)
    fetched = jnp.where(offset == 0, full_rows, jnp.zeros_like(full_rows))
    for stride in range(1, REACH + 1):
        for signed in (stride, -stride):
            arrived = from_behind(full_rows, "resp", signed)
            fetched = jnp.where(offset == signed, arrived, fetched)
    query_rows = queries[0, 0]
    resp_rows = resp_kv[0, 0]
    grad_rows = out_grad[0, 0]
    resp_len = query_rows.shape[0]
    row_index = jnp.arange(resp_len, dtype=jnp.int32)
    live_rows = row_index < lengths[0, 0] * BLOCK
    masked_grad = jnp.where(live_rows[:, None], grad_rows, jnp.zeros_like(grad_rows))
    causal = row_index[None, :] <= row_index[:, None]
    query_parts = []
    resp_key_parts = []
    resp_value_parts = []
    prompt_key_parts = []
    prompt_value_parts = []
    for head_index in range(KVH):
        query_slice = slice(head_index * groups * HD, (head_index + 1) * groups * HD)
        key_slice = slice(head_index * HD, (head_index + 1) * HD)
        value_slice = slice(key_width + head_index * HD, key_width + (head_index + 1) * HD)
        query_head_block = query_rows[:, query_slice].reshape(resp_len, groups, HD)
        head_gradient = masked_grad[:, query_slice].reshape(resp_len, groups, HD)
        prompt_key_block = fetched[:, key_slice]
        prompt_value_block = fetched[:, value_slice]
        response_key_block = resp_rows[:, key_slice]
        response_value_block = resp_rows[:, value_slice]
        score_resp = (
            jnp.einsum(
                "xjc,bc->jxb",
                query_head_block,
                response_key_block,
                preferred_element_type=jnp.float32,
            )
            * softmax_scale
        )
        score_resp = jnp.where(causal[None], score_resp, masked_value)
        score_prompt = (
            jnp.einsum(
                "xjc,bc->jxb",
                query_head_block,
                prompt_key_block,
                preferred_element_type=jnp.float32,
            )
            * softmax_scale
        )
        top_score = jnp.maximum(
            jnp.max(score_prompt, axis=-1, keepdims=True),
            jnp.max(score_resp, axis=-1, keepdims=True),
        )
        exp_prompt = jnp.exp(score_prompt - top_score)
        exp_resp = jnp.exp(score_resp - top_score)
        total_mass = jnp.sum(exp_prompt, axis=-1, keepdims=True) + jnp.sum(
            exp_resp, axis=-1, keepdims=True
        )
        prob_prompt = exp_prompt / total_mass
        prob_resp = exp_resp / total_mass
        prompt_round_block = prob_prompt.astype(jnp.bfloat16)
        response_round_block = prob_resp.astype(jnp.bfloat16)
        head_out = jnp.einsum(
            "czu,uk->zck",
            prompt_round_block,
            prompt_value_block,
            preferred_element_type=jnp.float32,
        )
        head_out = head_out + jnp.einsum(
            "czu,uk->zck",
            response_round_block,
            response_value_block,
            preferred_element_type=jnp.float32,
        )
        head_out = head_out.astype(jnp.bfloat16)
        row_delta = jnp.sum(
            head_gradient.astype(jnp.float32) * head_out.astype(jnp.float32), axis=-1
        )
        row_delta = jnp.transpose(row_delta, (1, 0))[..., None]
        back_prompt = jnp.einsum(
            "xjc,bc->jxb", head_gradient, prompt_value_block, preferred_element_type=jnp.float32
        )
        back_resp = jnp.einsum(
            "xjc,bc->jxb", head_gradient, response_value_block, preferred_element_type=jnp.float32
        )
        prompt_score_gradient = (prob_prompt * (back_prompt - row_delta)).astype(jnp.bfloat16)
        response_score_gradient = (prob_resp * (back_resp - row_delta)).astype(jnp.bfloat16)
        query_head_grad = jnp.einsum(
            "czu,uk->zck",
            prompt_score_gradient,
            prompt_key_block,
            preferred_element_type=jnp.float32,
        )
        query_head_grad = query_head_grad + jnp.einsum(
            "czu,uk->zck",
            response_score_gradient,
            response_key_block,
            preferred_element_type=jnp.float32,
        )
        query_parts.append(
            (query_head_grad * softmax_scale).astype(jnp.bfloat16).reshape(resp_len, groups * HD)
        )
        prompt_key_parts.append(
            jnp.einsum(
                "lpb,ply->by",
                prompt_score_gradient,
                query_head_block,
                preferred_element_type=jnp.float32,
            )
            * softmax_scale
        )
        prompt_value_parts.append(
            jnp.einsum(
                "lpb,ply->by", prompt_round_block, head_gradient, preferred_element_type=jnp.float32
            )
        )
        resp_key_parts.append(
            jnp.einsum(
                "lpb,ply->by",
                response_score_gradient,
                query_head_block,
                preferred_element_type=jnp.float32,
            )
            * softmax_scale
        )
        resp_value_parts.append(
            jnp.einsum(
                "lpb,ply->by",
                response_round_block,
                head_gradient,
                preferred_element_type=jnp.float32,
            )
        )
    query_grad = jnp.concatenate(query_parts, axis=1)
    resp_grad = jnp.concatenate(resp_key_parts + resp_value_parts, axis=1).astype(jnp.bfloat16)
    prompt_partial = jnp.concatenate(prompt_key_parts + prompt_value_parts, axis=1)
    rows_sum = lax.psum_scatter(prompt_partial, "prompt", scatter_dimension=0, tiled=True)
    collected = jnp.where(wanted == column, rows_sum, jnp.zeros_like(rows_sum))
    for stride in range(1, REACH + 1):
        for signed in (stride, -stride):
            arrived = from_behind(rows_sum.astype(jnp.bfloat16), "resp", -signed).astype(
                rows_sum.dtype
            )
            source = (column + signed + group_size) % group_size
            collected = collected + jnp.where(
                prompt_of[source] == column, arrived, jnp.zeros_like(arrived)
            )
    return (query_grad[None, None], resp_grad[None, None], collected[None])


def solution(mesh):
    return jax.shard_map(
        shards,
        mesh=mesh,
        in_specs=(
            P("prompt", "resp", None, None),
            P("prompt", "resp", None, None),
            P("prompt", "resp", None, None),
            P("resp", "prompt", None),
            P(),
            P("prompt", "resp"),
        ),
        out_specs=(
            P("prompt", "resp", None, None),
            P("prompt", "resp", None, None),
            P("resp", "prompt", None),
        ),
        check_vma=False,
    )
```

profile of v0, /device:TPU:199, one launch (start us, length us, event | category | flops | bytes accessed | tf_op | source)
XLA Modules:
  0.0 191.8 jit_solution(11302706265438290318)
XLA Ops:
  7.2 22.3 %all-gather = bf16[1,128,1024]{2,1,0:T(8,128)(2,1)} all-gather(bf16[1,16,1024]{2,1,0:T(8,128)(2,1)} %param.9), channel_id=2, replica_groups=mesh['prompt'=8,'resp'=64] {'prompt'}, dimensions={1}, use_global_device_ids=true | all-gather | bytes 294912 | tf_op jit(solution)/shard_map/all_gather | solution.py:29
  29.5 12.1 %collective-permute-start.5 = (bf16[128,1024]{1,0:T(8,128)(2,1)}, bf16[128,1024]{1,0:T(8,128)(2,1)}, u32[]{:S(2)}, u32[]{:S(2)}) collective-permute-start(bf16[128,1024]{1,0:T(8,128)(2,1)} %bitcast.1), channel_id=1, source_target_pairs={{0,1},{1,2},{2,3},{3,4},{4,5},{5,6},{6,7},{7,8},{8,9},{9,10},{10,1... | collective-permute-start | bytes 786440 | tf_op jit(solution)/shard_map/ppermute | solution.py:17
  41.6 1.9 %collective-permute-start.4 = (bf16[128,1024]{1,0:T(8,128)(2,1)}, bf16[128,1024]{1,0:T(8,128)(2,1)}, u32[]{:S(2)}, u32[]{:S(2)}) collective-permute-start(bf16[128,1024]{1,0:T(8,128)(2,1)} %bitcast.1), channel_id=1, source_target_pairs={{0,63},{1,0},{2,1},{3,2},{4,3},{5,4},{6,5},{7,6},{8,7},{9,8},{10,9... | collective-permute-start | bytes 786440 | tf_op jit(solution)/shard_map/ppermute | solution.py:17
  43.5 3.1 %collective-permute-start.3 = (bf16[128,1024]{1,0:T(8,128)(2,1)}, bf16[128,1024]{1,0:T(8,128)(2,1)}, u32[]{:S(2)}, u32[]{:S(2)}) collective-permute-start(bf16[128,1024]{1,0:T(8,128)(2,1)} %bitcast.1), channel_id=1, source_target_pairs={{0,2},{1,3},{2,4},{3,5},{4,6},{5,7},{6,8},{7,9},{8,10},{9,11},{10,... | collective-permute-start | bytes 786440 | tf_op jit(solution)/shard_map/ppermute | solution.py:17
  46.7 2.2 %collective-permute-start.2 = (bf16[128,1024]{1,0:T(8,128)(2,1)}, bf16[128,1024]{1,0:T(8,128)(2,1)}, u32[]{:S(2)}, u32[]{:S(2)}) collective-permute-start(bf16[128,1024]{1,0:T(8,128)(2,1)} %bitcast.1), channel_id=1, source_target_pairs={{0,62},{1,63},{2,0},{3,1},{4,2},{5,3},{6,4},{7,5},{8,6},{9,7},{10,... | collective-permute-start | bytes 786440 | tf_op jit(solution)/shard_map/ppermute | solution.py:17
  48.8 7.0 %collective-permute-start.1 = (bf16[128,1024]{1,0:T(8,128)(2,1)}, bf16[128,1024]{1,0:T(8,128)(2,1)}, u32[]{:S(2)}, u32[]{:S(2)}) collective-permute-start(bf16[128,1024]{1,0:T(8,128)(2,1)} %bitcast.1), channel_id=1, source_target_pairs={{0,3},{1,4},{2,5},{3,6},{4,7},{5,8},{6,9},{7,10},{8,11},{9,12},{10... | collective-permute-start | bytes 786440 | tf_op jit(solution)/shard_map/ppermute | solution.py:17
  56.6 1.5 copy.167
  58.1 0.9 fusion.140
  58.9 1.6 copy.170
  60.6 1.0 fusion.141
  61.6 1.1 fusion.144
  62.8 1.2 fusion.150
  64.0 0.7 fusion.142
  66.1 1.3 fusion.146
  67.4 2.1 %collective-permute-start = (bf16[128,1024]{1,0:T(8,128)(2,1)}, bf16[128,1024]{1,0:T(8,128)(2,1)}, u32[]{:S(2)}, u32[]{:S(2)}) collective-permute-start(bf16[128,1024]{1,0:T(8,128)(2,1)} %bitcast.1), channel_id=1, source_target_pairs={{0,61},{1,62},{2,63},{3,0},{4,1},{5,2},{6,3},{7,4},{8,5},{9,6},{10... | collective-permute-start | bytes 786440 | tf_op jit(solution)/shard_map/ppermute | solution.py:17
  73.1 1.3 fusion.148
  74.5 6.2 %collective-permute-done = bf16[128,1024]{1,0:T(8,128)(2,1)} collective-permute-done((bf16[128,1024]{1,0:T(8,128)(2,1)}, bf16[128,1024]{1,0:T(8,128)(2,1)}, u32[]{:S(2)}, u32[]{:S(2)}) %collective-permute-start) | collective-permute-done | bytes 262176 | tf_op jit(solution)/shard_map/ppermute | solution.py:17
  80.7 1.0 select_select_fusion
  82.2 0.5 copy-done
  83.6 0.7 copy-done.9
  85.2 0.3 fusion.16
  86.5 0.5 copy-done.19
  87.8 0.9 fusion.89
  89.7 0.5 copy-done.15
  90.5 0.3 fusion.17
  91.8 0.5 copy-done.17
  93.4 0.8 fusion.107
  94.2 1.0 fusion.50
  95.8 0.9 fusion.91
  96.7 1.0 fusion.48
  97.7 0.8 fusion.105
  98.5 1.0 fusion.46
  99.5 0.8 fusion.103
  100.3 1.0 fusion.44
  101.3 0.9 fusion.101
  102.1 0.9 fusion.99
  103.0 0.9 fusion.98
  103.9 0.9 fusion.97
  104.8 0.9 fusion.96
  105.7 2.1 %copy.327 = f32[128,1024]{1,0:T(8,128)} copy(f32[128,1024]{0,1:T(8,128)} %fusion.96) | data formatting | bytes 1048576
  107.8 0.9 fusion.93
  108.7 1.9 copy.224
  110.6 0.9 copy.221
  111.5 0.8 copy.223
  112.3 0.9 copy.222
  113.2 0.9 fusion.95
  114.2 0.9 fusion.87
  115.1 0.9 fusion.85
  116.1 1.1 maximum_bitcast_fusion
  117.2 24.7 %reduce-scatter.4.cloned.1.call-done = f32[16,1024]{1,0:T(8,128)} async-done(((f32[128,1024]{1,0:T(8,128)}), f32[16,1024]{1,0:T(8,128)}) %reduce-scatter.4.cloned.1.call-update) | async-done | bytes 65552
  141.9 1.0 copy.328
  142.9 10.9 %collective-permute-start.11 = (bf16[16,1024]{0,1:T(8,128)(2,1)S(1)}, bf16[16,1024]{0,1:T(8,128)(2,1)S(1)}, u32[]{:S(2)}, u32[]{:S(2)}) collective-permute-start(bf16[16,1024]{0,1:T(8,128)(2,1)S(1)} %convert_element_type.162), channel_id=1, source_target_pairs={{0,3},{1,4},{2,5},{3,6},{4,7},{5,8},{6,9},{7,10},{8,11},{9,12},{10... | collective-permute-start | bytes 98312 | tf_op jit(solution)/shard_map/ppermute | solution.py:17
  153.9 0.3 fusion.83
  154.2 1.9 %collective-permute-start.10 = (bf16[16,1024]{0,1:T(8,128)(2,1)S(1)}, bf16[16,1024]{0,1:T(8,128)(2,1)S(1)}, u32[]{:S(2)}, u32[]{:S(2)}) collective-permute-start(bf16[16,1024]{0,1:T(8,128)(2,1)S(1)} %convert_element_type.162), channel_id=1, source_target_pairs={{0,61},{1,62},{2,63},{3,0},{4,1},{5,2},{6,3},{7,4},{8,5},{9,6},{10... | collective-permute-start | bytes 98312 | tf_op jit(solution)/shard_map/ppermute | solution.py:17
  156.1 3.7 %collective-permute-start.9 = (bf16[16,1024]{0,1:T(8,128)(2,1)S(1)}, bf16[16,1024]{0,1:T(8,128)(2,1)S(1)}, u32[]{:S(2)}, u32[]{:S(2)}) collective-permute-start(bf16[16,1024]{0,1:T(8,128)(2,1)S(1)} %convert_element_type.162), channel_id=1, source_target_pairs={{0,2},{1,3},{2,4},{3,5},{4,6},{5,7},{6,8},{7,9},{8,10},{9,11},{10,... | collective-permute-start | bytes 98312 | tf_op jit(solution)/shard_map/ppermute | solution.py:17
  159.8 1.9 %collective-permute-start.8 = (bf16[16,1024]{0,1:T(8,128)(2,1)S(1)}, bf16[16,1024]{0,1:T(8,128)(2,1)S(1)}, u32[]{:S(2)}, u32[]{:S(2)}) collective-permute-start(bf16[16,1024]{0,1:T(8,128)(2,1)S(1)} %convert_element_type.162), channel_id=1, source_target_pairs={{0,62},{1,63},{2,0},{3,1},{4,2},{5,3},{6,4},{7,5},{8,6},{9,7},{10,... | collective-permute-start | bytes 98312 | tf_op jit(solution)/shard_map/ppermute | solution.py:17
  161.8 9.9 %collective-permute-start.7 = (bf16[16,1024]{0,1:T(8,128)(2,1)S(1)}, bf16[16,1024]{0,1:T(8,128)(2,1)S(1)}, u32[]{:S(2)}, u32[]{:S(2)}) collective-permute-start(bf16[16,1024]{0,1:T(8,128)(2,1)S(1)} %convert_element_type.162), channel_id=1, source_target_pairs={{0,1},{1,2},{2,3},{3,4},{4,5},{5,6},{6,7},{7,8},{8,9},{9,10},{10,1... | collective-permute-start | bytes 98312 | tf_op jit(solution)/shard_map/ppermute | solution.py:17
  171.6 1.9 %collective-permute-start.6 = (bf16[16,1024]{0,1:T(8,128)(2,1)S(1)}, bf16[16,1024]{0,1:T(8,128)(2,1)}, u32[]{:S(2)}, u32[]{:S(2)}) collective-permute-start(bf16[16,1024]{0,1:T(8,128)(2,1)S(1)} %convert_element_type.162), channel_id=1, source_target_pairs={{0,63},{1,0},{2,1},{3,2},{4,3},{5,4},{6,5},{7,6},{8,7},{9,8},{10,9... | collective-permute-start | bytes 98312 | tf_op jit(solution)/shard_map/ppermute | solution.py:17
  173.6 0.3 fusion.81
  173.9 1.0 copy.241
  174.9 0.7 copy-done.26
  175.6 7.1 %collective-permute-done.6 = bf16[16,1024]{0,1:T(8,128)(2,1)} collective-permute-done((bf16[16,1024]{0,1:T(8,128)(2,1)S(1)}, bf16[16,1024]{0,1:T(8,128)(2,1)}, u32[]{:S(2)}, u32[]{:S(2)}) %collective-permute-start.6) | collective-permute-done | bytes 32800 | tf_op jit(solution)/shard_map/ppermute | solution.py:17
  182.8 1.4 add_bitcast_fusion
  184.1 0.8 copy.242
  (108 shorter events, 8.0 us)
Async XLA Ops:
  7.2 134.7 %reduce-scatter.4.cloned.1.call-start = ((), (), s32[]{:S(2)}) async-start(), calls=%async_computation.1 | async-start | bytes 589824
  29.5 37.9 %collective-permute-start.5 = (bf16[128,1024]{1,0:T(8,128)(2,1)}, bf16[128,1024]{1,0:T(8,128)(2,1)}, u32[]{:S(2)}, u32[]{:S(2)}) collective-permute-start(bf16[128,1024]{1,0:T(8,128)(2,1)} %bitcast.1), channel_id=1, source_target_pairs={{0,1},{1,2},{2,3},{3,4},{4,5},{5,6},{6,7},{7,8},{8,9},{9,10},{10,1... | collective-permute-start | bytes 786440 | tf_op jit(solution)/shard_map/ppermute | solution.py:17
  41.6 32.8 %collective-permute-start.4 = (bf16[128,1024]{1,0:T(8,128)(2,1)}, bf16[128,1024]{1,0:T(8,128)(2,1)}, u32[]{:S(2)}, u32[]{:S(2)}) collective-permute-start(bf16[128,1024]{1,0:T(8,128)(2,1)} %bitcast.1), channel_id=1, source_target_pairs={{0,63},{1,0},{2,1},{3,2},{4,3},{5,4},{6,5},{7,6},{8,7},{9,8},{10,9... | collective-permute-start | bytes 786440 | tf_op jit(solution)/shard_map/ppermute | solution.py:17
  43.5 30.9 %collective-permute-start.3 = (bf16[128,1024]{1,0:T(8,128)(2,1)}, bf16[128,1024]{1,0:T(8,128)(2,1)}, u32[]{:S(2)}, u32[]{:S(2)}) collective-permute-start(bf16[128,1024]{1,0:T(8,128)(2,1)} %bitcast.1), channel_id=1, source_target_pairs={{0,2},{1,3},{2,4},{3,5},{4,6},{5,7},{6,8},{7,9},{8,10},{9,11},{10,... | collective-permute-start | bytes 786440 | tf_op jit(solution)/shard_map/ppermute | solution.py:17
  46.7 27.8 %collective-permute-start.2 = (bf16[128,1024]{1,0:T(8,128)(2,1)}, bf16[128,1024]{1,0:T(8,128)(2,1)}, u32[]{:S(2)}, u32[]{:S(2)}) collective-permute-start(bf16[128,1024]{1,0:T(8,128)(2,1)} %bitcast.1), channel_id=1, source_target_pairs={{0,62},{1,63},{2,0},{3,1},{4,2},{5,3},{6,4},{7,5},{8,6},{9,7},{10,... | collective-permute-start | bytes 786440 | tf_op jit(solution)/shard_map/ppermute | solution.py:17
  48.8 25.6 %collective-permute-start.1 = (bf16[128,1024]{1,0:T(8,128)(2,1)}, bf16[128,1024]{1,0:T(8,128)(2,1)}, u32[]{:S(2)}, u32[]{:S(2)}) collective-permute-start(bf16[128,1024]{1,0:T(8,128)(2,1)} %bitcast.1), channel_id=1, source_target_pairs={{0,3},{1,4},{2,5},{3,6},{4,7},{5,8},{6,9},{7,10},{8,11},{9,12},{10... | collective-permute-start | bytes 786440 | tf_op jit(solution)/shard_map/ppermute | solution.py:17
  58.9 3.8 %copy-start.3 = (bf16[256,512]{0,1:T(8,128)(2,1)}, bf16[256,512]{0,1:T(8,128)(2,1)S(1)}, u32[]{:S(2)}) copy-start(bf16[256,512]{0,1:T(8,128)(2,1)S(1)} %get-tuple-element.12) | copy-start | bytes 786436
  62.8 1.2 copy-start.27
  67.4 13.3 %collective-permute-start = (bf16[128,1024]{1,0:T(8,128)(2,1)}, bf16[128,1024]{1,0:T(8,128)(2,1)}, u32[]{:S(2)}, u32[]{:S(2)}) collective-permute-start(bf16[128,1024]{1,0:T(8,128)(2,1)} %bitcast.1), channel_id=1, source_target_pairs={{0,61},{1,62},{2,63},{3,0},{4,1},{5,2},{6,3},{7,4},{8,5},{9,6},{10... | collective-permute-start | bytes 786440 | tf_op jit(solution)/shard_map/ppermute | solution.py:17
  74.4 7.6 %copy-start.4 = (bf16[256,512]{0,1:T(8,128)(2,1)S(1)}, bf16[256,512]{0,1:T(8,128)(2,1)}, u32[]{:S(2)}) copy-start(bf16[256,512]{0,1:T(8,128)(2,1)} %copy-done.3) | copy-start | bytes 786436
  81.7 1.0 copy-start
  81.7 1.2 copy-start.2
  83.3 1.0 copy-start.9
  83.4 1.2 copy-start.13
  84.4 0.8 copy-start.5
  85.5 7.6 %copy-start.7 = (bf16[4,256,256]{1,2,0:T(8,128)(2,1)}, bf16[4,256,256]{1,2,0:T(8,128)(2,1)S(1)}, u32[]{:S(2)}) copy-start(bf16[4,256,256]{1,2,0:T(8,128)(2,1)S(1)} %fusion.16) | copy-start | bytes 1572868
  86.0 1.0 copy-start.19
  89.3 1.0 copy-start.15
  91.4 1.0 copy-start.17
  105.7 2.1 %copy-start.1 = (bf16[256,512]{0,1:T(8,128)(2,1)S(1)}, bf16[256,512]{0,1:T(8,128)(2,1)}, u32[]{:S(2)}) copy-start(bf16[256,512]{0,1:T(8,128)(2,1)} %get-tuple-element.14) | copy-start | bytes 786436
  107.7 2.9 %copy-start.10 = (bf16[256,4,128]{0,2,1:T(8,128)(2,1)S(1)}, bf16[256,4,128]{0,2,1:T(8,128)(2,1)}, u32[]{:S(2)}) copy-start(bf16[256,4,128]{0,2,1:T(8,128)(2,1)} %fusion.50) | copy-start | bytes 786436
  107.8 4.6 %copy-start.11 = (bf16[256,4,128]{0,2,1:T(8,128)(2,1)S(1)}, bf16[256,4,128]{0,2,1:T(8,128)(2,1)}, u32[]{:S(2)}) copy-start(bf16[256,4,128]{0,2,1:T(8,128)(2,1)} %fusion.48) | copy-start | bytes 786436
  108.7 2.8 %copy-start.12 = (bf16[256,4,128]{0,2,1:T(8,128)(2,1)S(1)}, bf16[256,4,128]{0,2,1:T(8,128)(2,1)}, u32[]{:S(2)}) copy-start(bf16[256,4,128]{0,2,1:T(8,128)(2,1)} %fusion.46) | copy-start | bytes 786436
  108.7 4.5 %copy-start.8 = (bf16[4,256,256]{1,2,0:T(8,128)(2,1)S(1)}, bf16[4,256,256]{1,2,0:T(8,128)(2,1)}, u32[]{:S(2)}) copy-start(bf16[4,256,256]{1,2,0:T(8,128)(2,1)} %copy-done.7) | copy-start | bytes 1572868
  111.5 2.7 %copy-start.20 = (bf16[256,512]{0,1:T(8,128)(2,1)S(1)}, bf16[256,512]{0,1:T(8,128)(2,1)}, u32[]{:S(2)}) copy-start(bf16[256,512]{0,1:T(8,128)(2,1)} %get-tuple-element.16) | copy-start | bytes 786436
  112.3 2.8 %copy-start.18 = (bf16[256,512]{0,1:T(8,128)(2,1)S(1)}, bf16[256,512]{0,1:T(8,128)(2,1)}, u32[]{:S(2)}) copy-start(bf16[256,512]{0,1:T(8,128)(2,1)} %get-tuple-element.19) | copy-start | bytes 786436
  114.1 1.9 copy-start.21
  114.1 1.9 copy-start.22
  114.1 1.9 copy-start.23
  114.1 1.9 copy-start.24
  116.1 37.8 %copy-start.25 = (bf16[1,1,256,1024]{2,3,1,0:T(8,128)(2,1)S(1)}, bf16[1,1,256,1024]{2,3,1,0:T(8,128)(2,1)}, u32[]{:S(2)}) copy-start(bf16[1,1,256,1024]{2,3,1,0:T(8,128)(2,1)} %fusion.85) | copy-start | bytes 1572868
  117.2 36.7 %copy-start.16 = (bf16[256,512]{0,1:T(8,128)(2,1)S(1)}, bf16[256,512]{0,1:T(8,128)(2,1)}, u32[]{:S(2)}) copy-start(bf16[256,512]{0,1:T(8,128)(2,1)} %get-tuple-element.18) | copy-start | bytes 786436
  117.2 56.4 %copy-start.6 = (bf16[4,256,256]{1,2,0:T(8,128)(2,1)S(1)}, bf16[4,256,256]{1,2,0:T(8,128)(2,1)}, u32[]{:S(2)}) copy-start(bf16[4,256,256]{1,2,0:T(8,128)(2,1)} %copy-done.5) | copy-start | bytes 1572868
  117.2 56.4 %copy-start.14 = (bf16[256,512]{0,1:T(8,128)(2,1)S(1)}, bf16[256,512]{0,1:T(8,128)(2,1)}, u32[]{:S(2)}) copy-start(bf16[256,512]{0,1:T(8,128)(2,1)} %get-tuple-element.17) | copy-start | bytes 786436
  142.9 28.7 %collective-permute-start.11 = (bf16[16,1024]{0,1:T(8,128)(2,1)S(1)}, bf16[16,1024]{0,1:T(8,128)(2,1)S(1)}, u32[]{:S(2)}, u32[]{:S(2)}) collective-permute-start(bf16[16,1024]{0,1:T(8,128)(2,1)S(1)} %convert_element_type.162), channel_id=1, source_target_pairs={{0,3},{1,4},{2,5},{3,6},{4,7},{5,8},{6,9},{7,10},{8,11},{9,12},{10... | collective-permute-start | bytes 98312 | tf_op jit(solution)/shard_map/ppermute | solution.py:17
  154.2 20.7 %collective-permute-start.10 = (bf16[16,1024]{0,1:T(8,128)(2,1)S(1)}, bf16[16,1024]{0,1:T(8,128)(2,1)S(1)}, u32[]{:S(2)}, u32[]{:S(2)}) collective-permute-start(bf16[16,1024]{0,1:T(8,128)(2,1)S(1)} %convert_element_type.162), channel_id=1, source_target_pairs={{0,61},{1,62},{2,63},{3,0},{4,1},{5,2},{6,3},{7,4},{8,5},{9,6},{10... | collective-permute-start | bytes 98312 | tf_op jit(solution)/shard_map/ppermute | solution.py:17
  156.1 18.8 %collective-permute-start.9 = (bf16[16,1024]{0,1:T(8,128)(2,1)S(1)}, bf16[16,1024]{0,1:T(8,128)(2,1)S(1)}, u32[]{:S(2)}, u32[]{:S(2)}) collective-permute-start(bf16[16,1024]{0,1:T(8,128)(2,1)S(1)} %convert_element_type.162), channel_id=1, source_target_pairs={{0,2},{1,3},{2,4},{3,5},{4,6},{5,7},{6,8},{7,9},{8,10},{9,11},{10,... | collective-permute-start | bytes 98312 | tf_op jit(solution)/shard_map/ppermute | solution.py:17
  159.8 15.1 %collective-permute-start.8 = (bf16[16,1024]{0,1:T(8,128)(2,1)S(1)}, bf16[16,1024]{0,1:T(8,128)(2,1)S(1)}, u32[]{:S(2)}, u32[]{:S(2)}) collective-permute-start(bf16[16,1024]{0,1:T(8,128)(2,1)S(1)} %convert_element_type.162), channel_id=1, source_target_pairs={{0,62},{1,63},{2,0},{3,1},{4,2},{5,3},{6,4},{7,5},{8,6},{9,7},{10,... | collective-permute-start | bytes 98312 | tf_op jit(solution)/shard_map/ppermute | solution.py:17
  161.8 13.2 %collective-permute-start.7 = (bf16[16,1024]{0,1:T(8,128)(2,1)S(1)}, bf16[16,1024]{0,1:T(8,128)(2,1)S(1)}, u32[]{:S(2)}, u32[]{:S(2)}) collective-permute-start(bf16[16,1024]{0,1:T(8,128)(2,1)S(1)} %convert_element_type.162), channel_id=1, source_target_pairs={{0,1},{1,2},{2,3},{3,4},{4,5},{5,6},{6,7},{7,8},{8,9},{9,10},{10,1... | collective-permute-start | bytes 98312 | tf_op jit(solution)/shard_map/ppermute | solution.py:17
  171.6 11.1 %collective-permute-start.6 = (bf16[16,1024]{0,1:T(8,128)(2,1)S(1)}, bf16[16,1024]{0,1:T(8,128)(2,1)}, u32[]{:S(2)}, u32[]{:S(2)}) collective-permute-start(bf16[16,1024]{0,1:T(8,128)(2,1)S(1)} %convert_element_type.162), channel_id=1, source_target_pairs={{0,63},{1,0},{2,1},{3,2},{4,3},{5,4},{6,5},{7,6},{8,7},{9,8},{10,9... | collective-permute-start | bytes 98312 | tf_op jit(solution)/shard_map/ppermute | solution.py:17
  174.9 0.7 copy-start.26
Sparse Core Ops, SparseCore 0:
  107.9 33.9 reduce-scatter.3
where the time goes:
time: 193 us; the launch traced here: 192 us
  starting transfers between devices  58.7 us (30%)
  waiting for transfers between devices  38.1 us (20%)
  matrix products  28.2 us (15%)
  blocking collectives  22.3 us (12%)
  between operations  20.5 us (11%)
  local copies, waits for them, and re-layouts  18.7 us (10%)
  other arithmetic  5.38 us (3%)
    ppermute x12, starting transfers between devices, from_behind(): return lax.ppermute(value, axis, pairs)  58.6 us
    unnamed x2, waiting for transfers between devices  24.7 us
    all_gather x1, blocking collectives, shards(): full_rows = lax.all_gather(own_rows, 'prompt', axis=0, tiled=True)  22.3 us
    ppermute x12, waiting for transfers between devices, from_behind(): return lax.ppermute(value, axis, pairs)  13.4 us
    unnamed x62, local copies, waits for them, and re-layouts  11.7 us
    dot_general x4, matrix products, shards(): jnp.einsum('xjc,bc->jxb', query_head_block, response_key_block, preferred...  4.9 us
    reshape x4, local copies, waits for them, and re-layouts, shards(): (query_head_grad * softmax_scale).astype(jnp.bfloat16)  4.45 us
  transfers between devices with their start and end apart: 13, of which 3 were waited for; matrix products, arithmetic and copies ran while one was open for 11% of the time, Pallas kernels for 0%

commit v1 on v0

--- a/solution.py
+++ b/solution.py
@@ -26,7 +26,9 @@
     wanted = prompt_of[column]
     offset = (column - wanted + group_size + REACH) % group_size - REACH
     own_rows = prompt_kv[0]
-    full_rows = lax.all_gather(own_rows, "prompt", axis=0, tiled=True)
+    full_rows = jnp.concatenate(
+        lax.all_to_all(jnp.stack([own_rows] * lax.axis_size("prompt")), "prompt", 0, 0), axis=0
+    )
     fetched = jnp.where(offset == 0, full_rows, jnp.zeros_like(full_rows))
     for stride in range(1, REACH + 1):
         for signed in (stride, -stride):

time: 193 us -> 173 us (0.90)
  blocking collectives: 22.3 us -> 0 us
  starting transfers between devices: 58.7 us -> 60.9 us
    all_gather x1 -> x0, blocking collectives: 22.3 us -> none  [shards(): full_rows = lax.all_gather(own_rows, 'prompt', axis=0, tiled=True)]
    all_to_all x0 -> x1, starting transfers between devices: none -> 6.82 us  [shards(): lax.all_to_all(jnp.stack([own_rows] * lax.axis_size('prompt')), 'prompt',...]
    ppermute x12, starting transfers between devices: 58.6 us -> 54 us  [from_behind(): return lax.ppermute(value, axis, pairs)]
    unnamed x2, waiting for transfers between devices: 24.7 us -> 20.2 us
    all_to_all x0 -> x1, waiting for transfers between devices: none -> 3.73 us  [shards(): lax.all_to_all(jnp.stack([own_rows] * lax.axis_size('prompt')), 'prompt',...]
    unnamed x62 -> x68, local copies, waits for them, and re-layouts: 11.7 us -> 10.9 us
  transfers between devices with their start and end apart: 13 -> 14, of which waited for: 3 -> 4; matrix products, arithmetic and copies ran while one was open for 11% -> 11% of each run, Pallas kernels for 0% -> 0%
where the time goes in v1:
time: 173 us; the launch traced here: 172 us
  starting transfers between devices  60.9 us (35%)
  waiting for transfers between devices  37.3 us (22%)
  matrix products  28.2 us (16%)
  between operations  20.7 us (12%)
  local copies, waits for them, and re-layouts  19.5 us (11%)
  other arithmetic  5.46 us (3%)
    ppermute x12, starting transfers between devices, from_behind(): return lax.ppermute(value, axis, pairs)  54 us
    unnamed x2, waiting for transfers between devices  20.2 us
    ppermute x12, waiting for transfers between devices, from_behind(): return lax.ppermute(value, axis, pairs)  13.4 us
    unnamed x68, local copies, waits for them, and re-layouts  10.9 us
    all_to_all x1, starting transfers between devices, shards(): lax.all_to_all(jnp.stack([own_rows] * lax.axis_size('prompt')), 'prompt',...  6.82 us
    dot_general x4, matrix products, shards(): jnp.einsum('xjc,bc->jxb', query_head_block, response_key_block, preferred...  4.9 us
    reshape x4, local copies, waits for them, and re-layouts, shards(): (query_head_grad * softmax_scale).astype(jnp.bfloat16)  4.45 us
    dot_general x4, matrix products, shards(): jnp.einsum('czu,uk->zck', prompt_score_gradient, prompt_key_block, prefer...  3.85 us
  transfers between devices with their start and end apart: 14, of which 4 were waited for; matrix products, arithmetic and copies ran while one was open for 11% of the time, Pallas kernels for 0%

profile of v1, /device:TPU:199, one launch (start us, length us, event | category | flops | bytes accessed | tf_op | source)
XLA Modules:
  0.0 172.0 jit_solution(13845226126004527993)
XLA Ops:
  7.2 1.6 stack.3
  8.7 6.8 %all-to-all-start = ((bf16[8,16,1024]{2,1,0:T(8,128)(2,1)}), bf16[8,16,1024]{2,1,0:T(8,128)(2,1)}, u32[]{:S(2)}, u32[]{:S(2)}) async-start(bf16[8,16,1024]{2,1,0:T(8,128)(2,1)} %stack.3), calls=%async_computation | async-start | bytes 524288 | tf_op jit(solution)/shard_map/all_to_all | solution.py:30
  16.4 0.5 copy.167
  16.9 0.9 fusion.140
  17.8 0.5 copy-done.11
  18.3 0.5 copy.170
  19.0 1.1 fusion.144
  20.1 1.0 fusion.141
  21.2 1.2 fusion.150
  22.3 3.7 %all-to-all-done = bf16[8,16,1024]{2,1,0:T(8,128)(2,1)} async-done(((bf16[8,16,1024]{2,1,0:T(8,128)(2,1)}), bf16[8,16,1024]{2,1,0:T(8,128)(2,1)}, u32[]{:S(2)}, u32[]{:S(2)}) %all-to-all-start) | async-done | bytes 262176 | tf_op jit(solution)/shard_map/all_to_all | solution.py:30
  26.0 7.5 %collective-permute-start.5 = (bf16[128,1024]{1,0:T(8,128)(2,1)}, bf16[128,1024]{1,0:T(8,128)(2,1)}, u32[]{:S(2)}, u32[]{:S(2)}) collective-permute-start(bf16[128,1024]{1,0:T(8,128)(2,1)} %bitcast.2), channel_id=1, source_target_pairs={{0,1},{1,2},{2,3},{3,4},{4,5},{5,6},{6,7},{7,8},{8,9},{9,10},{10,1... | collective-permute-start | bytes 786440 | tf_op jit(solution)/shard_map/ppermute | solution.py:17
  33.5 0.7 fusion.142
  35.5 1.3 fusion.146
  36.8 1.9 %collective-permute-start.4 = (bf16[128,1024]{1,0:T(8,128)(2,1)}, bf16[128,1024]{1,0:T(8,128)(2,1)}, u32[]{:S(2)}, u32[]{:S(2)}) collective-permute-start(bf16[128,1024]{1,0:T(8,128)(2,1)} %bitcast.2), channel_id=1, source_target_pairs={{0,63},{1,0},{2,1},{3,2},{4,3},{5,4},{6,5},{7,6},{8,7},{9,8},{10,9... | collective-permute-start | bytes 786440 | tf_op jit(solution)/shard_map/ppermute | solution.py:17
  38.7 3.1 %collective-permute-start.3 = (bf16[128,1024]{1,0:T(8,128)(2,1)}, bf16[128,1024]{1,0:T(8,128)(2,1)}, u32[]{:S(2)}, u32[]{:S(2)}) collective-permute-start(bf16[128,1024]{1,0:T(8,128)(2,1)} %bitcast.2), channel_id=1, source_target_pairs={{0,2},{1,3},{2,4},{3,5},{4,6},{5,7},{6,8},{7,9},{8,10},{9,11},{10,... | collective-permute-start | bytes 786440 | tf_op jit(solution)/shard_map/ppermute | solution.py:17
  41.8 2.2 %collective-permute-start.2 = (bf16[128,1024]{1,0:T(8,128)(2,1)}, bf16[128,1024]{1,0:T(8,128)(2,1)}, u32[]{:S(2)}, u32[]{:S(2)}) collective-permute-start(bf16[128,1024]{1,0:T(8,128)(2,1)} %bitcast.2), channel_id=1, source_target_pairs={{0,62},{1,63},{2,0},{3,1},{4,2},{5,3},{6,4},{7,5},{8,6},{9,7},{10,... | collective-permute-start | bytes 786440 | tf_op jit(solution)/shard_map/ppermute | solution.py:17
  44.0 7.0 %collective-permute-start.1 = (bf16[128,1024]{1,0:T(8,128)(2,1)}, bf16[128,1024]{1,0:T(8,128)(2,1)}, u32[]{:S(2)}, u32[]{:S(2)}) collective-permute-start(bf16[128,1024]{1,0:T(8,128)(2,1)} %bitcast.2), channel_id=1, source_target_pairs={{0,3},{1,4},{2,5},{3,6},{4,7},{5,8},{6,9},{7,10},{8,11},{9,12},{10... | collective-permute-start | bytes 786440 | tf_op jit(solution)/shard_map/ppermute | solution.py:17
  51.0 2.1 %collective-permute-start = (bf16[128,1024]{1,0:T(8,128)(2,1)}, bf16[128,1024]{1,0:T(8,128)(2,1)}, u32[]{:S(2)}, u32[]{:S(2)}) collective-permute-start(bf16[128,1024]{1,0:T(8,128)(2,1)} %bitcast.2), channel_id=1, source_target_pairs={{0,61},{1,62},{2,63},{3,0},{4,1},{5,2},{6,3},{7,4},{8,5},{9,6},{10... | collective-permute-start | bytes 786440 | tf_op jit(solution)/shard_map/ppermute | solution.py:17
  57.0 1.3 fusion.148
  58.4 6.9 %collective-permute-done = bf16[128,1024]{1,0:T(8,128)(2,1)} collective-permute-done((bf16[128,1024]{1,0:T(8,128)(2,1)}, bf16[128,1024]{1,0:T(8,128)(2,1)}, u32[]{:S(2)}, u32[]{:S(2)}) %collective-permute-start) | collective-permute-done | bytes 262176 | tf_op jit(solution)/shard_map/ppermute | solution.py:17
  65.3 1.0 select_select_fusion
  66.8 0.5 copy-done
  68.2 0.7 copy-done.9
  71.1 0.5 copy-done.21
  72.4 0.9 fusion.89
  74.3 0.5 copy-done.17
  76.4 0.5 copy-done.19
  78.0 0.8 fusion.107
  78.8 1.0 fusion.50
  80.3 0.9 fusion.91
  81.3 1.0 fusion.48
  82.3 0.8 fusion.105
  83.1 1.0 fusion.46
  84.1 0.8 fusion.103
  84.9 1.0 fusion.44
  85.9 0.9 fusion.101
  86.7 0.9 fusion.99
  87.6 0.9 fusion.98
  88.5 0.9 fusion.97
  89.4 0.9 fusion.96
  90.2 2.1 %copy.327 = f32[128,1024]{1,0:T(8,128)} copy(f32[128,1024]{0,1:T(8,128)} %fusion.96) | data formatting | bytes 1048576
  92.4 0.9 fusion.93
  93.3 1.9 %copy.224 = bf16[256,512]{1,0:T(8,128)(2,1)} copy(bf16[256,512]{0,1:T(8,128)(2,1)} %bitcast.552) | data formatting | bytes 524288 | tf_op jit(solution)/shard_map/reshape | solution.py:130
  95.2 0.9 copy.221
  96.1 0.8 copy.223
  96.9 0.9 copy.222
  97.8 0.9 fusion.95
  98.7 0.9 fusion.87
  99.7 0.9 fusion.85
  100.7 1.1 maximum_bitcast_fusion
  101.8 20.2 %reduce-scatter.4.cloned.1.call-done = f32[16,1024]{1,0:T(8,128)} async-done(((f32[128,1024]{1,0:T(8,128)}), f32[16,1024]{1,0:T(8,128)}) %reduce-scatter.4.cloned.1.call-update) | async-done | bytes 65552
  121.9 1.0 copy.328
  123.0 10.9 %collective-permute-start.11 = (bf16[16,1024]{0,1:T(8,128)(2,1)S(1)}, bf16[16,1024]{0,1:T(8,128)(2,1)S(1)}, u32[]{:S(2)}, u32[]{:S(2)}) collective-permute-start(bf16[16,1024]{0,1:T(8,128)(2,1)S(1)} %convert_element_type.162), channel_id=1, source_target_pairs={{0,3},{1,4},{2,5},{3,6},{4,7},{5,8},{6,9},{7,10},{8,11},{9,12},{10... | collective-permute-start | bytes 98312 | tf_op jit(solution)/shard_map/ppermute | solution.py:17
  134.3 1.9 %collective-permute-start.10 = (bf16[16,1024]{0,1:T(8,128)(2,1)S(1)}, bf16[16,1024]{0,1:T(8,128)(2,1)S(1)}, u32[]{:S(2)}, u32[]{:S(2)}) collective-permute-start(bf16[16,1024]{0,1:T(8,128)(2,1)S(1)} %convert_element_type.162), channel_id=1, source_target_pairs={{0,61},{1,62},{2,63},{3,0},{4,1},{5,2},{6,3},{7,4},{8,5},{9,6},{10... | collective-permute-start | bytes 98312 | tf_op jit(solution)/shard_map/ppermute | solution.py:17
  136.2 3.7 %collective-permute-start.9 = (bf16[16,1024]{0,1:T(8,128)(2,1)S(1)}, bf16[16,1024]{0,1:T(8,128)(2,1)S(1)}, u32[]{:S(2)}, u32[]{:S(2)}) collective-permute-start(bf16[16,1024]{0,1:T(8,128)(2,1)S(1)} %convert_element_type.162), channel_id=1, source_target_pairs={{0,2},{1,3},{2,4},{3,5},{4,6},{5,7},{6,8},{7,9},{8,10},{9,11},{10,... | collective-permute-start | bytes 98312 | tf_op jit(solution)/shard_map/ppermute | solution.py:17
  139.9 1.9 %collective-permute-start.8 = (bf16[16,1024]{0,1:T(8,128)(2,1)S(1)}, bf16[16,1024]{0,1:T(8,128)(2,1)S(1)}, u32[]{:S(2)}, u32[]{:S(2)}) collective-permute-start(bf16[16,1024]{0,1:T(8,128)(2,1)S(1)} %convert_element_type.162), channel_id=1, source_target_pairs={{0,62},{1,63},{2,0},{3,1},{4,2},{5,3},{6,4},{7,5},{8,6},{9,7},{10,... | collective-permute-start | bytes 98312 | tf_op jit(solution)/shard_map/ppermute | solution.py:17
  141.9 9.9 %collective-permute-start.7 = (bf16[16,1024]{0,1:T(8,128)(2,1)S(1)}, bf16[16,1024]{0,1:T(8,128)(2,1)S(1)}, u32[]{:S(2)}, u32[]{:S(2)}) collective-permute-start(bf16[16,1024]{0,1:T(8,128)(2,1)S(1)} %convert_element_type.162), channel_id=1, source_target_pairs={{0,1},{1,2},{2,3},{3,4},{4,5},{5,6},{6,7},{7,8},{8,9},{9,10},{10,1... | collective-permute-start | bytes 98312 | tf_op jit(solution)/shard_map/ppermute | solution.py:17
  151.8 1.9 %collective-permute-start.6 = (bf16[16,1024]{0,1:T(8,128)(2,1)S(1)}, bf16[16,1024]{0,1:T(8,128)(2,1)}, u32[]{:S(2)}, u32[]{:S(2)}) collective-permute-start(bf16[16,1024]{0,1:T(8,128)(2,1)S(1)} %convert_element_type.162), channel_id=1, source_target_pairs={{0,63},{1,0},{2,1},{3,2},{4,3},{5,4},{6,5},{7,6},{8,7},{9,8},{10,9... | collective-permute-start | bytes 98312 | tf_op jit(solution)/shard_map/ppermute | solution.py:17
  154.0 1.0 copy.241
  155.0 0.7 copy-done.28
  155.7 0.7 copy-done.29
  156.4 6.4 %collective-permute-done.6 = bf16[16,1024]{0,1:T(8,128)(2,1)} collective-permute-done((bf16[16,1024]{0,1:T(8,128)(2,1)S(1)}, bf16[16,1024]{0,1:T(8,128)(2,1)}, u32[]{:S(2)}, u32[]{:S(2)}) %collective-permute-start.6) | collective-permute-done | bytes 32800 | tf_op jit(solution)/shard_map/ppermute | solution.py:17
  162.9 1.4 add_bitcast_fusion
  164.3 0.8 copy.242
  (116 shorter events, 9.2 us)
Async XLA Ops:
  7.2 9.2 %copy-start.10 = (bf16[1,1,256,2048]{3,2,1,0:T(8,128)(2,1)S(1)}, bf16[1,1,256,2048]{3,2,1,0:T(8,128)(2,1)}, u32[]{:S(2)}) copy-start(bf16[1,1,256,2048]{3,2,1,0:T(8,128)(2,1)} %param.6) | copy-start | bytes 3145732
  8.7 17.3 %all-to-all-start = ((bf16[8,16,1024]{2,1,0:T(8,128)(2,1)}), bf16[8,16,1024]{2,1,0:T(8,128)(2,1)}, u32[]{:S(2)}, u32[]{:S(2)}) async-start(bf16[8,16,1024]{2,1,0:T(8,128)(2,1)} %stack.3), calls=%async_computation | async-start | bytes 524288 | tf_op jit(solution)/shard_map/all_to_all | solution.py:30
  15.6 106.4 %reduce-scatter.4.cloned.1.call-start = ((), (), s32[]{:S(2)}) async-start(), calls=%async_computation.2 | async-start | bytes 589824
  16.9 1.4 copy-start.11
  18.3 2.8 %copy-start.3 = (bf16[256,512]{0,1:T(8,128)(2,1)}, bf16[256,512]{0,1:T(8,128)(2,1)S(1)}, u32[]{:S(2)}) copy-start(bf16[256,512]{0,1:T(8,128)(2,1)S(1)} %get-tuple-element.12) | copy-start | bytes 786436
  21.2 12.4 %copy-start.30 = (s32[64]{0:T(128)S(1)}, s32[64]{0:T(128)}, u32[]{:S(2)}) copy-start(s32[64]{0:T(128)} %param.10) | copy-start | bytes 772
  26.0 24.9 %collective-permute-start.5 = (bf16[128,1024]{1,0:T(8,128)(2,1)}, bf16[128,1024]{1,0:T(8,128)(2,1)}, u32[]{:S(2)}, u32[]{:S(2)}) collective-permute-start(bf16[128,1024]{1,0:T(8,128)(2,1)} %bitcast.2), channel_id=1, source_target_pairs={{0,1},{1,2},{2,3},{3,4},{4,5},{5,6},{6,7},{7,8},{8,9},{9,10},{10,1... | collective-permute-start | bytes 786440 | tf_op jit(solution)/shard_map/ppermute | solution.py:17
  36.8 21.5 %collective-permute-start.4 = (bf16[128,1024]{1,0:T(8,128)(2,1)}, bf16[128,1024]{1,0:T(8,128)(2,1)}, u32[]{:S(2)}, u32[]{:S(2)}) collective-permute-start(bf16[128,1024]{1,0:T(8,128)(2,1)} %bitcast.2), channel_id=1, source_target_pairs={{0,63},{1,0},{2,1},{3,2},{4,3},{5,4},{6,5},{7,6},{8,7},{9,8},{10,9... | collective-permute-start | bytes 786440 | tf_op jit(solution)/shard_map/ppermute | solution.py:17
  38.7 19.6 %collective-permute-start.3 = (bf16[128,1024]{1,0:T(8,128)(2,1)}, bf16[128,1024]{1,0:T(8,128)(2,1)}, u32[]{:S(2)}, u32[]{:S(2)}) collective-permute-start(bf16[128,1024]{1,0:T(8,128)(2,1)} %bitcast.2), channel_id=1, source_target_pairs={{0,2},{1,3},{2,4},{3,5},{4,6},{5,7},{6,8},{7,9},{8,10},{9,11},{10,... | collective-permute-start | bytes 786440 | tf_op jit(solution)/shard_map/ppermute | solution.py:17
  41.8 16.5 %collective-permute-start.2 = (bf16[128,1024]{1,0:T(8,128)(2,1)}, bf16[128,1024]{1,0:T(8,128)(2,1)}, u32[]{:S(2)}, u32[]{:S(2)}) collective-permute-start(bf16[128,1024]{1,0:T(8,128)(2,1)} %bitcast.2), channel_id=1, source_target_pairs={{0,62},{1,63},{2,0},{3,1},{4,2},{5,3},{6,4},{7,5},{8,6},{9,7},{10,... | collective-permute-start | bytes 786440 | tf_op jit(solution)/shard_map/ppermute | solution.py:17
  44.0 14.3 %collective-permute-start.1 = (bf16[128,1024]{1,0:T(8,128)(2,1)}, bf16[128,1024]{1,0:T(8,128)(2,1)}, u32[]{:S(2)}, u32[]{:S(2)}) collective-permute-start(bf16[128,1024]{1,0:T(8,128)(2,1)} %bitcast.2), channel_id=1, source_target_pairs={{0,3},{1,4},{2,5},{3,6},{4,7},{5,8},{6,9},{7,10},{8,11},{9,12},{10... | collective-permute-start | bytes 786440 | tf_op jit(solution)/shard_map/ppermute | solution.py:17
  51.0 14.3 %collective-permute-start = (bf16[128,1024]{1,0:T(8,128)(2,1)}, bf16[128,1024]{1,0:T(8,128)(2,1)}, u32[]{:S(2)}, u32[]{:S(2)}) collective-permute-start(bf16[128,1024]{1,0:T(8,128)(2,1)} %bitcast.2), channel_id=1, source_target_pairs={{0,61},{1,62},{2,63},{3,0},{4,1},{5,2},{6,3},{7,4},{8,5},{9,6},{10... | collective-permute-start | bytes 786440 | tf_op jit(solution)/shard_map/ppermute | solution.py:17
  58.3 8.2 %copy-start.4 = (bf16[256,512]{0,1:T(8,128)(2,1)S(1)}, bf16[256,512]{0,1:T(8,128)(2,1)}, u32[]{:S(2)}) copy-start(bf16[256,512]{0,1:T(8,128)(2,1)} %copy-done.3) | copy-start | bytes 786436
  66.3 1.0 copy-start
  66.3 1.2 copy-start.2
  67.9 1.0 copy-start.9
  68.0 1.2 copy-start.15
  68.9 0.8 copy-start.5
  70.1 7.6 %copy-start.7 = (bf16[4,256,256]{1,2,0:T(8,128)(2,1)}, bf16[4,256,256]{1,2,0:T(8,128)(2,1)S(1)}, u32[]{:S(2)}) copy-start(bf16[4,256,256]{1,2,0:T(8,128)(2,1)S(1)} %fusion.16) | copy-start | bytes 1572868
  70.6 1.0 copy-start.21
  73.9 1.0 copy-start.17
  75.9 1.0 copy-start.19
  90.2 2.1 %copy-start.1 = (bf16[256,512]{0,1:T(8,128)(2,1)S(1)}, bf16[256,512]{0,1:T(8,128)(2,1)}, u32[]{:S(2)}) copy-start(bf16[256,512]{0,1:T(8,128)(2,1)} %get-tuple-element.14) | copy-start | bytes 786436
  92.3 2.9 %copy-start.12 = (bf16[256,4,128]{0,2,1:T(8,128)(2,1)S(1)}, bf16[256,4,128]{0,2,1:T(8,128)(2,1)}, u32[]{:S(2)}) copy-start(bf16[256,4,128]{0,2,1:T(8,128)(2,1)} %fusion.50) | copy-start | bytes 786436
  92.4 4.6 %copy-start.13 = (bf16[256,4,128]{0,2,1:T(8,128)(2,1)S(1)}, bf16[256,4,128]{0,2,1:T(8,128)(2,1)}, u32[]{:S(2)}) copy-start(bf16[256,4,128]{0,2,1:T(8,128)(2,1)} %fusion.48) | copy-start | bytes 786436
  93.3 2.8 %copy-start.14 = (bf16[256,4,128]{0,2,1:T(8,128)(2,1)S(1)}, bf16[256,4,128]{0,2,1:T(8,128)(2,1)}, u32[]{:S(2)}) copy-start(bf16[256,4,128]{0,2,1:T(8,128)(2,1)} %fusion.46) | copy-start | bytes 786436
  93.3 4.5 %copy-start.8 = (bf16[4,256,256]{1,2,0:T(8,128)(2,1)S(1)}, bf16[4,256,256]{1,2,0:T(8,128)(2,1)}, u32[]{:S(2)}) copy-start(bf16[4,256,256]{1,2,0:T(8,128)(2,1)} %copy-done.7) | copy-start | bytes 1572868
  96.1 2.7 %copy-start.22 = (bf16[256,512]{0,1:T(8,128)(2,1)S(1)}, bf16[256,512]{0,1:T(8,128)(2,1)}, u32[]{:S(2)}) copy-start(bf16[256,512]{0,1:T(8,128)(2,1)} %get-tuple-element.16) | copy-start | bytes 786436
  96.9 2.8 %copy-start.20 = (bf16[256,512]{0,1:T(8,128)(2,1)S(1)}, bf16[256,512]{0,1:T(8,128)(2,1)}, u32[]{:S(2)}) copy-start(bf16[256,512]{0,1:T(8,128)(2,1)} %get-tuple-element.19) | copy-start | bytes 786436
  98.7 1.9 %copy-start.23 = (bf16[256,512]{1,0:T(8,128)(2,1)S(1)}, bf16[256,512]{1,0:T(8,128)(2,1)}, u32[]{:S(2)}) copy-start(bf16[256,512]{1,0:T(8,128)(2,1)} %copy.224) | copy-start | bytes 786436
  98.7 1.9 %copy-start.24 = (bf16[256,512]{1,0:T(8,128)(2,1)S(1)}, bf16[256,512]{1,0:T(8,128)(2,1)}, u32[]{:S(2)}) copy-start(bf16[256,512]{1,0:T(8,128)(2,1)} %copy.221) | copy-start | bytes 786436
  98.7 1.9 %copy-start.25 = (bf16[256,512]{1,0:T(8,128)(2,1)S(1)}, bf16[256,512]{1,0:T(8,128)(2,1)}, u32[]{:S(2)}) copy-start(bf16[256,512]{1,0:T(8,128)(2,1)} %copy.223) | copy-start | bytes 786436
  98.7 1.9 %copy-start.26 = (bf16[256,512]{1,0:T(8,128)(2,1)S(1)}, bf16[256,512]{1,0:T(8,128)(2,1)}, u32[]{:S(2)}) copy-start(bf16[256,512]{1,0:T(8,128)(2,1)} %copy.222) | copy-start | bytes 786436
  100.6 33.3 %copy-start.27 = (bf16[1,1,256,1024]{2,3,1,0:T(8,128)(2,1)S(1)}, bf16[1,1,256,1024]{2,3,1,0:T(8,128)(2,1)}, u32[]{:S(2)}) copy-start(bf16[1,1,256,1024]{2,3,1,0:T(8,128)(2,1)} %fusion.85) | copy-start | bytes 1572868
  101.8 32.2 %copy-start.18 = (bf16[256,512]{0,1:T(8,128)(2,1)S(1)}, bf16[256,512]{0,1:T(8,128)(2,1)}, u32[]{:S(2)}) copy-start(bf16[256,512]{0,1:T(8,128)(2,1)} %get-tuple-element.18) | copy-start | bytes 786436
  101.8 51.9 %copy-start.6 = (bf16[4,256,256]{1,2,0:T(8,128)(2,1)S(1)}, bf16[4,256,256]{1,2,0:T(8,128)(2,1)}, u32[]{:S(2)}) copy-start(bf16[4,256,256]{1,2,0:T(8,128)(2,1)} %copy-done.5) | copy-start | bytes 1572868
  101.8 51.9 %copy-start.16 = (bf16[256,512]{0,1:T(8,128)(2,1)S(1)}, bf16[256,512]{0,1:T(8,128)(2,1)}, u32[]{:S(2)}) copy-start(bf16[256,512]{0,1:T(8,128)(2,1)} %get-tuple-element.17) | copy-start | bytes 786436
  123.0 28.7 %collective-permute-start.11 = (bf16[16,1024]{0,1:T(8,128)(2,1)S(1)}, bf16[16,1024]{0,1:T(8,128)(2,1)S(1)}, u32[]{:S(2)}, u32[]{:S(2)}) collective-permute-start(bf16[16,1024]{0,1:T(8,128)(2,1)S(1)} %convert_element_type.162), channel_id=1, source_target_pairs={{0,3},{1,4},{2,5},{3,6},{4,7},{5,8},{6,9},{7,10},{8,11},{9,12},{10... | collective-permute-start | bytes 98312 | tf_op jit(solution)/shard_map/ppermute | solution.py:17
  134.3 20.7 %collective-permute-start.10 = (bf16[16,1024]{0,1:T(8,128)(2,1)S(1)}, bf16[16,1024]{0,1:T(8,128)(2,1)S(1)}, u32[]{:S(2)}, u32[]{:S(2)}) collective-permute-start(bf16[16,1024]{0,1:T(8,128)(2,1)S(1)} %convert_element_type.162), channel_id=1, source_target_pairs={{0,61},{1,62},{2,63},{3,0},{4,1},{5,2},{6,3},{7,4},{8,5},{9,6},{10... | collective-permute-start | bytes 98312 | tf_op jit(solution)/shard_map/ppermute | solution.py:17
  136.2 18.8 %collective-permute-start.9 = (bf16[16,1024]{0,1:T(8,128)(2,1)S(1)}, bf16[16,1024]{0,1:T(8,128)(2,1)S(1)}, u32[]{:S(2)}, u32[]{:S(2)}) collective-permute-start(bf16[16,1024]{0,1:T(8,128)(2,1)S(1)} %convert_element_type.162), channel_id=1, source_target_pairs={{0,2},{1,3},{2,4},{3,5},{4,6},{5,7},{6,8},{7,9},{8,10},{9,11},{10,... | collective-permute-start | bytes 98312 | tf_op jit(solution)/shard_map/ppermute | solution.py:17
  139.9 15.1 %collective-permute-start.8 = (bf16[16,1024]{0,1:T(8,128)(2,1)S(1)}, bf16[16,1024]{0,1:T(8,128)(2,1)S(1)}, u32[]{:S(2)}, u32[]{:S(2)}) collective-permute-start(bf16[16,1024]{0,1:T(8,128)(2,1)S(1)} %convert_element_type.162), channel_id=1, source_target_pairs={{0,62},{1,63},{2,0},{3,1},{4,2},{5,3},{6,4},{7,5},{8,6},{9,7},{10,... | collective-permute-start | bytes 98312 | tf_op jit(solution)/shard_map/ppermute | solution.py:17
  141.9 13.2 %collective-permute-start.7 = (bf16[16,1024]{0,1:T(8,128)(2,1)S(1)}, bf16[16,1024]{0,1:T(8,128)(2,1)S(1)}, u32[]{:S(2)}, u32[]{:S(2)}) collective-permute-start(bf16[16,1024]{0,1:T(8,128)(2,1)S(1)} %convert_element_type.162), channel_id=1, source_target_pairs={{0,1},{1,2},{2,3},{3,4},{4,5},{5,6},{6,7},{7,8},{8,9},{9,10},{10,1... | collective-permute-start | bytes 98312 | tf_op jit(solution)/shard_map/ppermute | solution.py:17
  151.8 11.1 %collective-permute-start.6 = (bf16[16,1024]{0,1:T(8,128)(2,1)S(1)}, bf16[16,1024]{0,1:T(8,128)(2,1)}, u32[]{:S(2)}, u32[]{:S(2)}) collective-permute-start(bf16[16,1024]{0,1:T(8,128)(2,1)S(1)} %convert_element_type.162), channel_id=1, source_target_pairs={{0,63},{1,0},{2,1},{3,2},{4,3},{5,4},{6,5},{7,6},{8,7},{9,8},{10,9... | collective-permute-start | bytes 98312 | tf_op jit(solution)/shard_map/ppermute | solution.py:17
  155.0 0.7 copy-start.28
  155.7 0.7 copy-start.29
Sparse Core Ops, SparseCore 0:
  92.5 29.4 reduce-scatter.3
